TPU v7x, 32 devices: a whole 2x2x4 slice. The times are simulated.
32 devices in a mesh: req: 8 (over z, x), sub: 4 (over y, core).
Axes of the slice: x: 2, y: 2, z: 4, core: 2. Of those that a mesh axis runs over, the one named last changes fastest.
Arguments:
- tokens: bfloat16 [4096, 2048], P(('req', 'sub')), may hold values from -6 to 6
- attn_gain: float32 [2048], replicated, may hold values from 0.25 to 1.75
- w_query: bfloat16 [2048, 1536], replicated, may hold values from -0.125 to 0.125
- w_latent: bfloat16 [2048, 576], replicated, may hold values from -0.125 to 0.125
- latent_gain: float32 [512], replicated, may hold values from 0.25 to 1.75
- w_key_up: bfloat16 [8, 128, 512], replicated, may hold values from -0.5 to 0.5
- w_value_up: bfloat16 [8, 512, 128], replicated, may hold values from -0.25 to 0.25
- w_out: bfloat16 [1024, 2048], replicated, may hold values from -0.1875 to 0.1875
- moe_gain: float32 [2048], replicated, may hold values from 0.25 to 1.75
- w_gate: bfloat16 [32, 2048, 704], P(('req', 'sub')), may hold values from -0.125 to 0.125
- w_up: bfloat16 [32, 2048, 704], P(('req', 'sub')), may hold values from -0.125 to 0.125
- w_down: bfloat16 [32, 704, 2048], P(('req', 'sub')), may hold values from -0.15625 to 0.15625
- expert_ids: int32 [4096, 6], P(('req', 'sub')), may hold values from 0 to 15, all different within a row; in each aligned block of 128 rows (0 to 127, 128 to 255, ...) at most 64 rows name the same one
- gate_weights: float32 [4096, 6], P(('req', 'sub')), may hold values from 0.1 to 0.6
- lengths: int32 [8, 3], P('req'), may hold values from 1 to 256, 512 in all within a row
- slab_group: int32 [8], P('req'), may hold values from 0 to 3
- owners: int32 [4], replicated, may hold values from 0 to 7, as said below
- prefix_pool: bfloat16 [8, 1024, 576], P('req'), as said below
Outputs:
- hidden_out: bfloat16 [4096, 2048], P(('req', 'sub'))
- new_cache: bfloat16 [4096, 576], P(('req', 'sub'))
Inputs may be any that keep to these rules, and one draw needn't show every extreme that they name: `expert_ids`: each row names 6 different experts; in each aligned block of 128 rows (the rows of one device) no expert is named by more than 64 rows, and in some block one expert is named by exactly 64 rows. Each slab's 3 lengths sum to 512, and its longest request has exactly half of 512 tokens. 4 distinct slots, among them slot 0 and slot 7; group g's cached prefix is prefix_pool[owners[g]]. `prefix_pool`: each row holds 512 latent entries followed by 64 rotary key entries.
All inputs are finite; a program needn't handle non-finite values.
Results may differ from a plain program's by a relative error of at most 0.013.
The roundings to bfloat16 on the way count: a program that leaves them out, or rounds other values in their place, can miss the bound.
Values may be sent and summed in bfloat16 or wider, within the bound.
A program may use at most 128 MiB of HBM per device.

v0:
```python
import jax
import jax.numpy as jnp
from jax import lax
from jax.sharding import PartitionSpec as P

EPSILON = 1e-06
FLOOR_SCORE = -1e30


def from_root(x, axis, root):
    mine = lax.axis_index(axis) == root
    return lax.psum(jnp.where(mine, x, jnp.zeros_like(x)), axis)


def rms_scale(values, gain):
    return values * lax.rsqrt(jnp.mean(values * values, axis=-1, keepdims=True) + EPSILON) * gain


def angle_tables(positions, rope_width):
    half_width = rope_width // 2
    inverse = 10000.0 ** (-jnp.arange(half_width, dtype=jnp.float32) / half_width)
    angles = positions.astype(jnp.float32)[:, None] * inverse[None, :]
    return (jnp.cos(angles), jnp.sin(angles))


def rotate(values, cos_part, sin_part):
    half_width = values.shape[-1] // 2
    first_half = values[..., :half_width]
    second = values[..., half_width:]
    return jnp.concatenate(
        [first_half * cos_part - second * sin_part, second * cos_part + first_half * sin_part],
        axis=-1,
    )


def slab_layout(req_lengths, slab_rows):
    req_count = req_lengths.shape[0]
    order = jnp.arange(req_count, dtype=jnp.int32)
    req_ends = jnp.sum(jnp.where(order[None, :] <= order[:, None], req_lengths[None, :], 0), axis=1)
    req_starts = req_ends - req_lengths
    slab_pos = jnp.arange(slab_rows, dtype=jnp.int32)
    segment = jnp.sum((slab_pos[:, None] >= req_ends[None, :]).astype(jnp.int32), axis=1)
    member_of = segment[:, None] == jnp.arange(req_lengths.shape[0], dtype=jnp.int32)[None, :]
    seg_start = jnp.sum(jnp.where(member_of, req_starts[None, :], 0), axis=1)
    return (slab_pos, segment, slab_pos - seg_start)


def block_attend(running, query_full, key_rows, allowed, score_scale, lat_width):
    row_top, denominator, weighted = running
    scores = (
        jnp.einsum("thc,kc->thk", query_full, key_rows, preferred_element_type=jnp.float32)
        * score_scale
    )
    scores = jnp.where(allowed[:, None, :], scores, FLOOR_SCORE)
    new_top = jnp.maximum(row_top, jnp.max(scores, axis=2))
    weights = jnp.where(allowed[:, None, :], jnp.exp(scores - new_top[:, :, None]), 0.0)
    rescale = jnp.exp(row_top - new_top)
    denominator = denominator * rescale + jnp.sum(weights, axis=2)
    weighted = weighted * rescale[:, :, None] + jnp.einsum(
        "thk,kc->thc",
        weights.astype(jnp.bfloat16),
        key_rows[:, :lat_width],
        preferred_element_type=jnp.float32,
    )
    return (new_top, denominator, weighted)


def route_tables(expert_ids, gate_weights, expert_count):
    experts = jnp.arange(expert_count, dtype=jnp.int32)
    named = expert_ids[:, :, None] == experts[None, None, :]
    chosen_of = jnp.sum(named.astype(jnp.float32), axis=1)
    gate_of = jnp.sum(jnp.where(named, gate_weights[:, :, None], 0.0), axis=1)
    return (chosen_of, gate_of)


def expert_half(slot_rows, gate_half, up_half, down_half):
    gate_proj = jnp.dot(slot_rows, gate_half, preferred_element_type=jnp.float32)
    up_proj = jnp.dot(slot_rows, up_half, preferred_element_type=jnp.float32)
    activated = (jax.nn.silu(gate_proj) * up_proj).astype(jnp.bfloat16)
    return jnp.dot(activated, down_half, preferred_element_type=jnp.float32)


def local(
    tokens,
    attn_gain,
    w_query,
    w_latent,
    latent_gain,
    w_key_up,
    w_value_up,
    w_out,
    moe_gain,
    w_gate,
    w_up,
    w_down,
    expert_ids,
    gate_weights,
    lengths,
    slab_group,
    owners,
    prefix_pool,
):
    rows_dev, model_width = tokens.shape
    head_count, nope_width, lat_width = w_key_up.shape
    rope_width = w_latent.shape[1] - lat_width
    prefix_len = prefix_pool.shape[1]
    sub_count = lax.axis_size("sub")
    device_count = lax.axis_size("req") * sub_count
    sub_index = lax.axis_index("sub")
    slab_rows = rows_dev * sub_count
    slab_pos, segment, offset = slab_layout(lengths[0], slab_rows)
    own_first = sub_index * rows_dev
    own_pos = lax.dynamic_slice_in_dim(slab_pos, own_first, rows_dev)
    own_seg = lax.dynamic_slice_in_dim(segment, own_first, rows_dev)
    own_offset = lax.dynamic_slice_in_dim(offset, own_first, rows_dev)
    cos_part, sin_part = angle_tables(prefix_len + own_offset, rope_width)
    normed = rms_scale(tokens.astype(jnp.float32), attn_gain).astype(jnp.bfloat16)
    latent = jnp.dot(normed, w_latent, preferred_element_type=jnp.float32)
    cache_rows = jnp.concatenate(
        [
            rms_scale(latent[:, :lat_width], latent_gain),
            rotate(latent[:, lat_width:], cos_part, sin_part),
        ],
        axis=1,
    ).astype(jnp.bfloat16)
    queries = jnp.dot(normed, w_query, preferred_element_type=jnp.float32).astype(jnp.bfloat16)
    queries = queries.reshape(rows_dev, head_count, nope_width + rope_width)
    query_lat = jnp.einsum(
        "thj,hjc->thc", queries[:, :, :nope_width], w_key_up, preferred_element_type=jnp.float32
    )
    query_rot = rotate(
        queries[:, :, nope_width:].astype(jnp.float32), cos_part[:, None, :], sin_part[:, None, :]
    )
    query_full = jnp.concatenate([query_lat, query_rot], axis=2).astype(jnp.bfloat16)
    score_scale = (nope_width + rope_width) ** (-0.5)
    my_group = slab_group[0]
    start_state = (
        jnp.full((rows_dev, head_count), FLOOR_SCORE, dtype=jnp.float32),
        jnp.zeros((rows_dev, head_count), dtype=jnp.float32),
        jnp.zeros((rows_dev, head_count, lat_width), dtype=jnp.float32),
    )
    local_prefix = prefix_pool[0]
    prefix = jnp.zeros_like(local_prefix)
    for member in range(owners.shape[0]):
        copied = from_root(local_prefix, "req", owners[member])
        prefix = jnp.where(my_group == member, copied, prefix)
    everyone = jnp.ones((rows_dev, prefix_len), dtype=bool)
    running = block_attend(start_state, query_full, prefix, everyone, score_scale, lat_width)
    key_block = lax.all_gather(cache_rows, "sub", axis=0, tiled=True)
    block_len = key_block.shape[0]
    key_pos = jnp.arange(block_len, dtype=jnp.int32)
    allowed = (segment[None, :] == own_seg[:, None]) & (key_pos[None, :] <= own_pos[:, None])
    running = block_attend(running, query_full, key_block, allowed, score_scale, lat_width)
    row_top, denominator, weighted = running
    latent_out = (weighted / denominator[:, :, None]).astype(jnp.bfloat16)
    head_out = jnp.einsum(
        "thc,hcv->thv", latent_out, w_value_up, preferred_element_type=jnp.float32
    ).astype(jnp.bfloat16)
    head_out = head_out.reshape(rows_dev, head_count * w_value_up.shape[2])
    residual = tokens.astype(jnp.float32) + jnp.dot(
        head_out, w_out, preferred_element_type=jnp.float32
    )
    normed_mid = rms_scale(residual, moe_gain).astype(jnp.bfloat16)
    top_count = expert_ids.shape[1]
    expert_count = device_count // 2
    capacity = 4 * rows_dev * top_count // (3 * expert_count)
    chosen_of, gate_of = route_tables(expert_ids, gate_weights, expert_count)
    row_order = jnp.arange(rows_dev, dtype=jnp.int32)
    earlier = (row_order[None, :] < row_order[:, None]).astype(jnp.bfloat16)
    slot_of = jnp.dot(earlier, chosen_of.astype(jnp.bfloat16), preferred_element_type=jnp.float32)
    slots = jnp.arange(capacity, dtype=jnp.float32)
    at_slot = (slot_of[:, :, None] == slots[None, None, :]) & (chosen_of[:, :, None] > 0.0)
    placing = at_slot.astype(jnp.bfloat16).reshape(rows_dev, expert_count * capacity)
    mixing = jnp.where(at_slot, gate_of[:, :, None], 0.0).reshape(rows_dev, expert_count * capacity)
    outbound = jnp.einsum(
        "ts,td->sd", placing, normed_mid, preferred_element_type=jnp.float32
    ).astype(jnp.bfloat16)
    doubled = jnp.broadcast_to(
        outbound.reshape(expert_count, 1, capacity, model_width),
        (expert_count, 2, capacity, model_width),
    )
    arrived = lax.all_to_all(
        doubled.reshape(device_count, capacity, model_width),
        ("req", "sub"),
        split_axis=0,
        concat_axis=0,
        tiled=True,
    )
    partial_value = expert_half(arrived.reshape(-1, model_width), w_gate[0], w_up[0], w_down[0])
    returned = lax.all_to_all(
        partial_value.reshape(device_count, capacity, model_width).astype(jnp.bfloat16),
        ("req", "sub"),
        split_axis=0,
        concat_axis=0,
        tiled=True,
    ).astype(jnp.float32)
    merged = returned.reshape(expert_count, 2, capacity, model_width)
    expert_out = (merged[:, 0] + merged[:, 1]).astype(jnp.bfloat16)
    expert_flat = expert_out.reshape(-1, model_width)
    mixing_high = mixing.astype(jnp.bfloat16)
    mixing_low = (mixing - mixing_high.astype(jnp.float32)).astype(jnp.bfloat16)
    routed_sum = jnp.dot(mixing_high, expert_flat, preferred_element_type=jnp.float32) + jnp.dot(
        mixing_low, expert_flat, preferred_element_type=jnp.float32
    )
    hidden_out = (residual + routed_sum).astype(jnp.bfloat16)
    return (hidden_out, cache_rows)


def solution(mesh):
    in_specs = (
        P(("req", "sub"), None),
        P(),
        P(),
        P(),
        P(),
        P(),
        P(),
        P(),
        P(),
        P(("req", "sub"), None, None),
        P(("req", "sub"), None, None),
        P(("req", "sub"), None, None),
        P(("req", "sub"), None),
        P(("req", "sub"), None),
        P("req", None),
        P("req"),
        P(),
        P("req", None, None),
    )
    out_specs = (P(("req", "sub"), None), P(("req", "sub"), None))
    return jax.shard_map(local, mesh=mesh, in_specs=in_specs, out_specs=out_specs, check_vma=False)
```

profile of v0, /device:TPU:0, one launch (start us, length us, event | category | flops | bytes accessed | tf_op | source)
XLA Modules:
  0.0 665.2 jit_solution(18293505204057355194)
XLA Ops:
  7.2 1.5 fusion.64
  11.2 2.4 copy.47
  13.6 3.8 select_bitcast_fusion
  19.9 2.5 fusion.48
  25.3 5.5 convolution_convert_fusion.2
  30.8 2.0 copy.42
  32.8 0.9 slice.64
  34.5 1.8 convert_element_type.112
  38.7 1.0 multiply_reduce_fusion.2
  39.8 1.1 multiply_convert_fusion.3
  41.6 8.4 %all_gather.3 = bf16[512,576]{0,1:T(8,128)(2,1)S(1)} all-gather(bf16[128,576]{0,1:T(8,128)(2,1)S(1)} %pad_maximum_fusion.3), channel_id=1, replica_groups=mesh['req'=8,'sub'=4] {'sub'}, dimensions={0}, use_global_device_ids=true | all-gather | bytes 737280 | tf_op jit(solution)/shard_map/all_gather | solution.py:149
  50.8 1.1 subtract_convert_fusion
  53.6 2.9 fusion.13
  56.5 148.9 %all-reduce.3.cloned.1.call-done = (bf16[1024,576]{1,0:T(8,128)(2,1)}, bf16[1024,576]{1,0:T(8,128)(2,1)}, bf16[1024,576]{1,0:T(8,128)(2,1)}, bf16[1024,576]{1,0:T(8,128)(2,1)}) async-done(((bf16[1024,576]{1,0:T(8,128)(2,1)}, bf16[1024,576]{1,0:T(8,128)(2,1)}, bf16[1024,576]{1,0:T(8,128)(2,1)}, bf16[1024,576]{1,0:T(8,128)(2,1)}), (bf16[1024,576]{1,0:T(8,128)(2,1)}, bf16[1024,576]{1,0:T(8,128)(2,1)}, ...) | async-done | bytes 4718608 | tf_op jit(solution)/shard_map/psum | solution.py:12
  205.4 1.7 select_select_fusion
  207.2 1.9 multiply_reduce_fusion
  209.1 0.9 fusion.1
  210.0 2.6 fusion.9
  213.4 5.0 fusion.20
  218.4 3.1 multiply_reduce_fusion.1
  221.6 3.3 convolution_convert_fusion.1
  224.9 6.8 %broadcast_in_dim.149 = bf16[16,2,64,2048]{3,2,1,0:T(8,128)(2,1)} broadcast(bf16[16,64,2048]{2,1,0:T(8,128)(2,1)} %bitcast.88), dimensions={0,2,3} | broadcast | bytes 12582912 | tf_op jit(solution)/shard_map/broadcast_in_dim | solution.py:178
  231.6 187.0 %all_to_all.10 = bf16[32,64,2048]{2,1,0:T(8,128)(2,1)S(1)} all-to-all(bf16[32,64,2048]{2,1,0:T(8,128)(2,1)} %bitcast.87), channel_id=1, replica_groups=mesh['req'=8,'sub'=4] {'req','sub'}, dimensions={0} | all-to-all | bytes 16777216 | tf_op jit(solution)/shard_map/all_to_all | solution.py:182
  418.6 6.3 fusion.5
  424.9 8.2 %multiply_convert_fusion = bf16[2048,704]{0,1:T(8,128)(2,1)} fusion(f32[2048,704]{0,1:T(8,128)S(1)} %fusion.5, bf16[2048,2048]{1,0:T(8,128)(2,1)S(1)} %bitcast.90, bf16[1,2048,704]{1,2,0:T(8,128)(2,1)S(1)} %copy-done.33), kind=kOutput, calls=%fused_computation.2 | convolution fusion | flops 5914230784 | bytes 19922944 | tf_op jit(solution)/shard_map/dot_general | solution.py:78
  433.1 4.7 copy.56
  437.7 10.9 %convolution_convert_fusion = bf16[32,64,2048]{2,1,0:T(8,128)(2,1)} fusion(bf16[32,64,704]{2,1,0:T(8,128)(2,1)} %bitcast.91, bf16[1,704,2048]{2,1,0:T(8,128)(2,1)S(1)} %copy-done), kind=kOutput, calls=%fused_computation.3 | convolution fusion | flops 5909774336 | bytes 14155776 | tf_op jit(solution)/shard_map/dot_general | solution.py:80
  448.6 4.2 all-to-all-start.1
  453.1 184.7 %all-to-all-done.1 = bf16[32,64,2048]{2,1,0:T(8,128)(2,1)} async-done(((bf16[32,64,2048]{2,1,0:T(8,128)(2,1)}), bf16[32,64,2048]{2,1,0:T(8,128)(2,1)}, u32[]{:S(2)}, u32[]{:S(2)}) %all-to-all-start.1) | async-done | bytes 8388640 | tf_op jit(solution)/shard_map/all_to_all | solution.py:190
  637.9 11.2 %convert.26 = f32[16,2,64,2048]{3,2,1,0:T(8,128)} convert(bf16[16,2,64,2048]{3,2,1,0:T(8,128)(2,1)} %bitcast.35) | non-fusion elementwise | flops 4194304 | bytes 25165824 | tf_op jit(solution)/shard_map/reshape | solution.py:197
  649.1 6.5 fusion
  656.8 1.5 fusion.8
  (105 shorter events, 13.3 us)
Async XLA Ops:
  7.2 430.6 %copy-start = (bf16[1,704,2048]{2,1,0:T(8,128)(2,1)S(1)}, bf16[1,704,2048]{2,1,0:T(8,128)(2,1)}, u32[]{:S(2)}) copy-start(bf16[1,704,2048]{2,1,0:T(8,128)(2,1)} %param.29) | copy-start | bytes 8650756
  7.2 198.3 %all-reduce.3.cloned.1.call-start = ((), (), s32[]{:S(2)}) async-start(), calls=%async_computation.2 | async-start | bytes 10485760 | tf_op jit(solution)/shard_map/psum | solution.py:12
  17.4 2.3 copy-start.3
  17.4 2.5 copy-start.25
  18.3 1.6 copy-start.26
  25.3 11.7 %copy-start.29 = (s32[128,6]{0,1:T(8,128)S(1)}, s32[128,6]{0,1:T(8,128)}, u32[]{:S(2)}) copy-start(s32[128,6]{0,1:T(8,128)} %param.30) | copy-start | bytes 9220
  25.3 11.7 %copy-start.30 = (f32[128,6]{0,1:T(8,128)S(1)}, f32[128,6]{0,1:T(8,128)}, u32[]{:S(2)}) copy-start(f32[128,6]{0,1:T(8,128)} %param.31) | copy-start | bytes 9220
  30.8 8.9 %copy-start.31 = (f32[512]{0:T(512)S(1)}, f32[512]{0:T(512)}, u32[]{:S(2)}) copy-start(f32[512]{0:T(512)} %param.22) | copy-start | bytes 6148
  37.1 13.8 %copy-start.4 = (f32[128,8,64]{2,0,1:T(8,128)S(1)}, f32[128,8,64]{2,0,1:T(8,128)}, u32[]{:S(2)}) copy-start(f32[128,8,64]{2,0,1:T(8,128)} %convert_element_type.112) | copy-start | bytes 786436
  37.1 14.9 %copy-start.7 = (bf16[128,1536]{0,1:T(8,128)(2,1)S(1)}, bf16[128,1536]{0,1:T(8,128)(2,1)}, u32[]{:S(2)}) copy-start(bf16[128,1536]{0,1:T(8,128)(2,1)} %copy.42) | copy-start | bytes 1179652
  37.1 14.9 %copy-start.8 = (bf16[8,128,512]{2,1,0:T(8,128)(2,1)S(1)}, bf16[8,128,512]{2,1,0:T(8,128)(2,1)}, u32[]{:S(2)}) copy-start(bf16[8,128,512]{2,1,0:T(8,128)(2,1)} %param.23) | copy-start | bytes 3145732
  37.7 2.0 copy-start.23
  37.8 1.9 copy-start.21
  41.6 14.9 %copy-start.12 = (bf16[128,576]{0,1:T(8,128)(2,1)}, bf16[128,576]{0,1:T(8,128)(2,1)S(1)}, u32[]{:S(2)}) copy-start(bf16[128,576]{0,1:T(8,128)(2,1)S(1)} %pad_maximum_fusion.3) | copy-start | bytes 442372
  50.0 2.5 copy-start.11
  50.8 1.7 copy-start.14
  205.4 1.7 copy-start.10
  205.4 1.7 copy-start.17
  205.4 1.7 copy-start.19
  207.2 1.9 copy-start.27
  210.0 2.7 copy-start.6
  210.0 2.7 copy-start.15
  218.4 3.2 copy-start.13
  218.4 3.2 copy-start.28
  221.5 3.3 copy-start.1
  231.6 187.0 %copy-start.32 = (bf16[1,2048,704]{1,2,0:T(8,128)(2,1)S(1)}, bf16[1,2048,704]{1,2,0:T(8,128)(2,1)}, u32[]{:S(2)}) copy-start(bf16[1,2048,704]{1,2,0:T(8,128)(2,1)} %param.27) | copy-start | bytes 8650756
  418.6 6.3 copy-start.33
  448.6 4.3 copy-start.20
  448.6 4.3 copy-start.22
  448.6 4.3 copy-start.24
  448.6 189.3 %all-to-all-start.1 = ((bf16[32,64,2048]{2,1,0:T(8,128)(2,1)}), bf16[32,64,2048]{2,1,0:T(8,128)(2,1)}, u32[]{:S(2)}, u32[]{:S(2)}) async-start(bf16[32,64,2048]{2,1,0:T(8,128)(2,1)} %convolution_convert_fusion), calls=%async_computation.1 | async-start | bytes 16777216 | tf_op jit(solution)/shard_map/all_to_all | solution.py:190
  655.6 1.2 copy-start.2
  (5 other events, 3.9 us)
Sparse Core Ops, SparseCore 0:
  17.5 187.8 all-reduce.2
where the time goes:
time: 668 us; the launch traced here: 665 us
  waiting for transfers between devices  334 us (50%)
  blocking collectives  195 us (29%)
  matrix products  55 us (8%)
  other arithmetic  34.5 us (5%)
  local copies, waits for them, and re-layouts  24.8 us (4%)
  between operations  17.6 us (3%)
    all_to_all x1, blocking collectives, local(): lax.all_to_all(doubled.reshape(device_count, capacity, model_width), ('re...  187 us
    all_to_all x1, waiting for transfers between devices, local(): lax.all_to_all(partial_value.reshape(device_count, capacity, model_width)...  185 us
    psum x1, waiting for transfers between devices, from_root(): return lax.psum(jnp.where(mine, x, jnp.zeros_like(x)), axis)  149 us
  transfers between devices with their start and end apart: 2, of which 2 were waited for; matrix products, arithmetic and copies ran while one was open for 4% of the time, Pallas kernels for 0%

commit v1 on v0

--- a/solution.py
+++ b/solution.py
@@ -7,9 +7,18 @@
 FLOOR_SCORE = -1e30
 
 
-def from_root(x, axis, root):
-    mine = lax.axis_index(axis) == root
-    return lax.psum(jnp.where(mine, x, jnp.zeros_like(x)), axis)
+def swap_cores(x):
+    pairs = [(i, i + 1 - 2 * (i % 2)) for i in range(lax.axis_size("sub"))]
+    return lax.ppermute(x, "sub", pairs)
+
+
+def group_prefix(prefix_pool, owner):
+    sub_count = lax.axis_size("sub")
+    share = prefix_pool.shape[1] // sub_count
+    mine = lax.dynamic_slice_in_dim(prefix_pool[0], lax.axis_index("sub") * share, share)
+    every = lax.all_gather(mine, "req", axis=0)
+    picked = lax.dynamic_index_in_dim(every, owner, 0, keepdims=False)
+    return lax.all_gather(picked, "sub", axis=0, tiled=True)
 
 
 def rms_scale(values, gain):
@@ -73,11 +82,10 @@
     return (chosen_of, gate_of)
 
 
-def expert_half(slot_rows, gate_half, up_half, down_half):
+def hidden_half(slot_rows, gate_half, up_half):
     gate_proj = jnp.dot(slot_rows, gate_half, preferred_element_type=jnp.float32)
     up_proj = jnp.dot(slot_rows, up_half, preferred_element_type=jnp.float32)
-    activated = (jax.nn.silu(gate_proj) * up_proj).astype(jnp.bfloat16)
-    return jnp.dot(activated, down_half, preferred_element_type=jnp.float32)
+    return (jax.nn.silu(gate_proj) * up_proj).astype(jnp.bfloat16)
 
 
 def local(
@@ -108,6 +116,9 @@
     device_count = lax.axis_size("req") * sub_count
     sub_index = lax.axis_index("sub")
     slab_rows = rows_dev * sub_count
+    gate_other = swap_cores(w_gate[0])
+    up_other = swap_cores(w_up[0])
+    down_other = swap_cores(w_down[0])
     slab_pos, segment, offset = slab_layout(lengths[0], slab_rows)
     own_first = sub_index * rows_dev
     own_pos = lax.dynamic_slice_in_dim(slab_pos, own_first, rows_dev)
@@ -139,11 +150,7 @@
         jnp.zeros((rows_dev, head_count), dtype=jnp.float32),
         jnp.zeros((rows_dev, head_count, lat_width), dtype=jnp.float32),
     )
-    local_prefix = prefix_pool[0]
-    prefix = jnp.zeros_like(local_prefix)
-    for member in range(owners.shape[0]):
-        copied = from_root(local_prefix, "req", owners[member])
-        prefix = jnp.where(my_group == member, copied, prefix)
+    prefix = group_prefix(prefix_pool, owners[my_group])
     everyone = jnp.ones((rows_dev, prefix_len), dtype=bool)
     running = block_attend(start_state, query_full, prefix, everyone, score_scale, lat_width)
     key_block = lax.all_gather(cache_rows, "sub", axis=0, tiled=True)
@@ -175,27 +182,28 @@
     outbound = jnp.einsum(
         "ts,td->sd", placing, normed_mid, preferred_element_type=jnp.float32
     ).astype(jnp.bfloat16)
-    doubled = jnp.broadcast_to(
-        outbound.reshape(expert_count, 1, capacity, model_width),
-        (expert_count, 2, capacity, model_width),
-    )
+    core_groups = [list(range(core, device_count, 2)) for core in range(2)]
     arrived = lax.all_to_all(
-        doubled.reshape(device_count, capacity, model_width),
+        outbound.reshape(expert_count, capacity, model_width),
         ("req", "sub"),
         split_axis=0,
         concat_axis=0,
+        axis_index_groups=core_groups,
         tiled=True,
-    )
-    partial_value = expert_half(arrived.reshape(-1, model_width), w_gate[0], w_up[0], w_down[0])
-    returned = lax.all_to_all(
-        partial_value.reshape(device_count, capacity, model_width).astype(jnp.bfloat16),
+    ).reshape(-1, model_width)
+    expert_rows = jnp.dot(
+        hidden_half(arrived, w_gate[0], w_up[0]), w_down[0], preferred_element_type=jnp.float32
+    ) + jnp.dot(
+        hidden_half(arrived, gate_other, up_other), down_other, preferred_element_type=jnp.float32
+    )
+    expert_out = lax.all_to_all(
+        expert_rows.astype(jnp.bfloat16).reshape(expert_count, capacity, model_width),
         ("req", "sub"),
         split_axis=0,
         concat_axis=0,
+        axis_index_groups=core_groups,
         tiled=True,
-    ).astype(jnp.float32)
-    merged = returned.reshape(expert_count, 2, capacity, model_width)
-    expert_out = (merged[:, 0] + merged[:, 1]).astype(jnp.bfloat16)
+    )
     expert_flat = expert_out.reshape(-1, model_width)
     mixing_high = mixing.astype(jnp.bfloat16)
     mixing_low = (mixing - mixing_high.astype(jnp.float32)).astype(jnp.bfloat16)

time: 668 us -> 359 us (0.54)
  waiting for transfers between devices: 334 us -> 127 us
  blocking collectives: 195 us -> 126 us
  other arithmetic: 34.5 us -> 6.88 us
  local copies, waits for them, and re-layouts: 24.8 us -> 7.04 us
  matrix products: 55 us -> 68.7 us
    psum x1 -> x0, waiting for transfers between devices: 149 us -> none  [from_root(): return lax.psum(jnp.where(mine, x, jnp.zeros_like(x)), axis)]
    all_to_all x1, waiting for transfers between devices: 185 us -> 80.2 us  [local(): lax.all_to_all(outbound.reshape(expert_count, capacity, model_width), ('r...]
    all_to_all x1, blocking collectives: 187 us -> 118 us  [local(): lax.all_to_all(expert_rows.astype(jnp.bfloat16).reshape(expert_count, cap...]
    all_gather x0 -> x2, waiting for transfers between devices: none -> 46.4 us  [the longest x1 41.9 us: group_prefix(): every = lax.all_gather(mine, 'req', axis=0)]
    dot_general x3 -> x4, matrix products: 25.3 us -> 41.9 us  [the longest x2 15.7 us: hidden_half(): jnp.dot(slot_rows, gate_half, preferred_element_type=jnp.float32)]
    reshape x1 -> x0, other arithmetic: 11.2 us -> none  [local(): merged = returned.reshape(expert_count, 2, capacity, model_width)]
    convert_element_type x3 -> x0, other arithmetic: 6.76 us -> none  [the longest x1 6.5 us: local(): expert_out = (merged[:, 0] + merged[:, 1]).astype(jnp.bfloat16)]
    broadcast_in_dim x1 -> x0, local copies, waits for them, and re-layouts: 6.76 us -> none  [local(): jnp.broadcast_to(outbound.reshape(expert_count, 1, capacity, model_width)...]
  transfers between devices with their start and end apart: 2 -> 6, of which waited for: 2 -> 3; matrix products, arithmetic and copies ran while one was open for 4% -> 12% of each run, Pallas kernels for 0% -> 0%
where the time goes in v1:
time: 359 us; the launch traced here: 358 us
  waiting for transfers between devices  127 us (35%)
  blocking collectives  126 us (35%)
  matrix products  68.7 us (19%)
  between operations  17 us (5%)
  local copies, waits for them, and re-layouts  7.04 us (2%)
  other arithmetic  6.88 us (2%)
  starting transfers between devices  6.41 us (2%)
    all_to_all x1, blocking collectives, local(): lax.all_to_all(expert_rows.astype(jnp.bfloat16).reshape(expert_count, cap...  118 us
    all_to_all x1, waiting for transfers between devices, local(): lax.all_to_all(outbound.reshape(expert_count, capacity, model_width), ('r...  80.2 us
    all_gather x1, waiting for transfers between devices, group_prefix(): every = lax.all_gather(mine, 'req', axis=0)  41.9 us
    dot_general x2, matrix products, hidden_half(): jnp.dot(slot_rows, gate_half, preferred_element_type=jnp.float32)  15.7 us
    dot_general x1, matrix products, local(): jnp.dot(hidden_half(arrived, gate_other, up_other), down_other, preferred...  13.6 us
    dot_general x1, matrix products, local(): jnp.dot(hidden_half(arrived, w_gate[0], w_up[0]), w_down[0], preferred_el...  12.6 us
    all_gather x1, blocking collectives, local(): key_block = lax.all_gather(cache_rows, 'sub', axis=0, tiled=True)  7.71 us
  transfers between devices with their start and end apart: 6, of which 3 were waited for; matrix products, arithmetic and copies ran while one was open for 12% of the time, Pallas kernels for 0%

profile of v1, /device:TPU:0, one launch (start us, length us, event | category | flops | bytes accessed | tf_op | source)
XLA Modules:
  0.0 358.5 jit_solution(16723735242241116761)
XLA Ops:
  7.3 1.8 constant_dynamic-slice_fusion
  9.8 1.2 dynamic_slice.21
  13.0 0.8 select_reduce_fusion.2
  13.9 0.7 fusion.60
  14.7 1.3 select_reduce_fusion
  16.0 1.2 fusion.20
  17.3 1.9 fusion.55
  19.6 4.0 %convolution_convert_fusion.1 = bf16[128,1536]{1,0:T(8,128)(2,1)S(1)} fusion(bf16[2048,1536]{1,0:T(8,128)(2,1)} %param.20, bf16[128,2048]{1,0:T(8,128)(2,1)S(1)} %copy-done.2, f32[2048]{0:T(1024)S(1)} %copy-done.15, f32[128]{0:T(128)S(1)} %add_rsqrt_fusion.2), kind=kOutput, calls=%fused_computation.14 | convolution fusion | flops 806551552 | bytes 7217664 | tf_op jit(solution)/shard_map/dot_general | solution.py:137
  23.7 41.9 %all-gather.4.cloned.1.call-done = bf16[8,256,576]{1,2,0:T(8,128)(2,1)} async-done(((bf16[1,256,576]{1,2,0:T(8,128)(2,1)}), bf16[8,256,576]{1,2,0:T(8,128)(2,1)}) %all-gather.4.cloned.1.call-update) | async-done | bytes 2359312 | tf_op jit(solution)/shard_map/all_gather | solution.py:19
  65.6 1.7 constant_dynamic-slice_fusion.1
  68.7 7.7 %all_gather.12 = bf16[512,576]{0,1:T(8,128)(2,1)S(1)} all-gather(bf16[128,576]{0,1:T(8,128)(2,1)S(1)} %pad_maximum_fusion.3), channel_id=1, replica_groups=mesh['req'=8,'sub'=4] {'sub'}, dimensions={0}, use_global_device_ids=true | all-gather | bytes 737280 | tf_op jit(solution)/shard_map/all_gather | solution.py:156
  76.8 0.5 fusion.13
  77.6 0.7 copy-done.6
  78.3 1.1 fusion.9
  79.4 4.5 %all-gather.6.cloned.1.call-done = bf16[1,1024,576]{1,2,0:T(8,128)(2,1)} async-done(((bf16[1,256,576]{1,2,0:T(8,128)(2,1)}), bf16[1,1024,576]{1,2,0:T(8,128)(2,1)}) %all-gather.6.cloned.1.call-update) | async-done | bytes 1179664 | tf_op jit(solution)/shard_map/all_gather | solution.py:21
  83.9 3.6 %multiply_reduce_fusion = (f32[128,8]{0,1:T(8,128)S(1)}, f32[128,8,1024]{2,0,1:T(8,128)S(1)}) fusion(bf16[1,1024,576]{1,2,0:T(8,128)(2,1)} %all-gather.6.cloned.1.call-done, bf16[128,8,32]{2,0,1:T(8,128)(2,1)} %copy-done.9, bf16[128,8,32]{2,0,1:T(8,128)(2,1)} %copy-done.8, bf16[128,8,512]{2,0,1:T(8,128)(2,1)} %copy-done.6), kind=kOutput, calls=%fused_computation.2 | convolution fusion | flops 1213594624 | bytes 6557696 | tf_op jit(solution)/shard_map/thc,kc->thk/dot_general | solution.py:60
  87.5 0.9 fusion
  88.8 2.6 fusion.5
  91.4 0.7 fusion.10
  92.1 4.2 %fusion.15 = bf16[8,128,128]{1,2,0:T(8,128)(2,1)S(1)} fusion(bf16[8,512,128]{2,1,0:T(8,128)(2,1)} %param.24, f32[128,8,512]{2,0,1:T(8,128)} %fusion.5, f32[128,8,512]{2,0,1:T(8,128)} %copy-done.4, f32[128,8]{0,1:T(8,128)S(1)} %get-tuple-element.4, f32[128,8]{0,1:T(8,128)S(1)} %get-tuple-element.11, f32[128,8]{0,1:T(8,128)S(1)} %get-tuple-element.5, ...), kind=kOutput, calls=%fused_computation.31 | convolution fusion | flops 676462592 | bytes 6111232 | tf_op jit(solution)/shard_map/thc,hcv->thv/dot_general | solution.py:163
  96.3 3.0 multiply_reduce_fusion.1
  99.4 3.3 convolution_convert_fusion
  102.6 5.7 %all-to-all-start = ((bf16[16,64,2048]{2,1,0:T(8,128)(2,1)}), bf16[16,64,2048]{2,1,0:T(8,128)(2,1)}, u32[]{:S(2)}, u32[]{:S(2)}) async-start(bf16[16,64,2048]{2,1,0:T(8,128)(2,1)} %bitcast.81), calls=%async_computation | async-start | bytes 8388608 | tf_op jit(solution)/shard_map/all_to_all | solution.py:186
  108.4 0.5 collective-permute-start.2
  109.0 80.2 %all-to-all-done = bf16[16,64,2048]{2,1,0:T(8,128)(2,1)} async-done(((bf16[16,64,2048]{2,1,0:T(8,128)(2,1)}), bf16[16,64,2048]{2,1,0:T(8,128)(2,1)}, u32[]{:S(2)}, u32[]{:S(2)}) %all-to-all-start) | async-done | bytes 4194336 | tf_op jit(solution)/shard_map/all_to_all | solution.py:186
  189.2 7.8 %fusion.66 = f32[1024,704]{0,1:T(8,128)} fusion(bf16[1024,2048]{1,0:T(8,128)(2,1)} %bitcast.17, bf16[1,2048,704]{1,2,0:T(8,128)(2,1)} %param.27), kind=kOutput, calls=%fused_computation.113 | convolution fusion | flops 2952790016 | bytes 9961472 | tf_op jit(solution)/shard_map/dot_general | solution.py:86
  197.0 7.9 %fusion.82 = f32[1024,704]{0,1:T(8,128)} fusion(bf16[1024,2048]{1,0:T(8,128)(2,1)} %bitcast.17, bf16[2048,704]{0,1:T(8,128)(2,1)} %collective-permute-done), kind=kOutput, calls=%fused_computation.125 | convolution fusion | flops 2952790016 | bytes 9961472 | tf_op jit(solution)/shard_map/dot_general | solution.py:86
  204.9 12.6 %fusion.36 = f32[1024,2048]{1,0:T(8,128)} fusion(f32[1024,704]{0,1:T(8,128)} %fusion.66, bf16[1024,2048]{1,0:T(8,128)(2,1)} %bitcast.17, bf16[1,704,2048]{2,1,0:T(8,128)(2,1)} %param.29, bf16[1,2048,704]{1,2,0:T(8,128)(2,1)} %param.28), kind=kOutput, calls=%fused_computation.48 | convolution fusion | flops 5909905408 | bytes 21233664 | tf_op jit(solution)/shard_map/dot_general | solution.py:194
  217.5 13.6 %add_convert_fusion = bf16[1024,2048]{1,0:T(8,128)(2,1)} fusion(f32[1024,2048]{1,0:T(8,128)} %fusion.36, bf16[704,2048]{1,0:T(8,128)(2,1)} %collective-permute-done.2, f32[1024,704]{0,1:T(8,128)} %fusion.82, bf16[1024,2048]{1,0:T(8,128)(2,1)} %bitcast.17, bf16[2048,704]{0,1:T(8,128)(2,1)} %collective-permute-done.1), kind=kOutput, calls=%fused_computation | convolution fusion | flops 5914099712 | bytes 25427968 | tf_op jit(solution)/shard_map/dot_general | solution.py:196
  231.1 118.1 %all_to_all.10 = bf16[16,64,2048]{2,1,0:T(8,128)(2,1)S(1)} all-to-all(bf16[16,64,2048]{2,1,0:T(8,128)(2,1)} %bitcast.82), channel_id=1, replica_groups={{0,2,4,6,8,10,12,14,16,18,20,22,24,26,28,30},{1,3,5,7,9,11,13,15,17,19,..., dimensions={0} | all-to-all | bytes 8388608 | tf_op jit(solution)/shard_map/all_to_all | solution.py:199
  349.2 0.8 convolution_bitcast_fusion
  350.1 1.6 fusion.4
  (80 shorter events, 3.3 us)
Async XLA Ops:
  7.2 10.1 %copy-start = (bf16[2048,576]{0,1:T(8,128)(2,1)S(1)}, bf16[2048,576]{0,1:T(8,128)(2,1)}, u32[]{:S(2)}) copy-start(bf16[2048,576]{0,1:T(8,128)(2,1)} %param.21) | copy-start | bytes 7077892
  7.2 12.4 %copy-start.2 = (bf16[128,2048]{1,0:T(8,128)(2,1)S(1)}, bf16[128,2048]{1,0:T(8,128)(2,1)}, u32[]{:S(2)}) copy-start(bf16[128,2048]{1,0:T(8,128)(2,1)} %param.18) | copy-start | bytes 1572868
  7.2 12.4 %copy-start.15 = (f32[2048]{0:T(1024)S(1)}, f32[2048]{0:T(1024)}, u32[]{:S(2)}) copy-start(f32[2048]{0:T(1024)} %param.19) | copy-start | bytes 24580
  7.2 58.4 %all-gather.4.cloned.1.call-start = ((), (), s32[]{:S(2)}) async-start(), calls=%async_computation.2 | async-start | bytes 2654208 | tf_op jit(solution)/shard_map/all_gather | solution.py:19
  9.1 74.8 %all-gather.6.cloned.1.call-start = ((), (), s32[]{:S(2)}) async-start(), calls=%async_computation.3 | async-start | bytes 1474560 | tf_op jit(solution)/shard_map/all_gather | solution.py:21
  13.9 53.4 %copy-start.16 = (s32[512]{0:T(512)}, s32[512]{0:T(512)S(1)}, u32[]{:S(2)}) copy-start(s32[512]{0:T(512)S(1)} %convert_reduce_fusion.1) | copy-start | bytes 6148
  19.3 49.0 %copy-start.13 = (pred[128,16]{0,1:T(8,128)(4,1)}, pred[128,16]{0,1:T(8,128)(4,1)S(1)}, u32[]{:S(2)}) copy-start(pred[128,16]{0,1:T(8,128)(4,1)S(1)} %broadcast_compare_fusion) | copy-start | bytes 6148
  19.4 48.8 %copy-start.11 = (f32[128,16]{0,1:T(8,128)}, f32[128,16]{0,1:T(8,128)S(1)}, u32[]{:S(2)}) copy-start(f32[128,16]{0,1:T(8,128)S(1)} %fusion.58) | copy-start | bytes 24580
  23.6 44.8 %copy-start.19 = (f32[512]{0:T(512)S(1)}, f32[512]{0:T(512)}, u32[]{:S(2)}) copy-start(f32[512]{0:T(512)} %param.22) | copy-start | bytes 6148
  67.4 9.0 %copy-start.17 = (s32[512]{0:T(512)S(1)}, s32[512]{0:T(512)}, u32[]{:S(2)}) copy-start(s32[512]{0:T(512)} %copy-done.16) | copy-start | bytes 6148
  67.5 9.3 %copy-start.5 = (bf16[8,128,512]{2,1,0:T(8,128)(2,1)S(1)}, bf16[8,128,512]{2,1,0:T(8,128)(2,1)}, u32[]{:S(2)}) copy-start(bf16[8,128,512]{2,1,0:T(8,128)(2,1)} %param.23) | copy-start | bytes 3145732
  68.7 10.8 %copy-start.7 = (bf16[128,576]{0,1:T(8,128)(2,1)}, bf16[128,576]{0,1:T(8,128)(2,1)S(1)}, u32[]{:S(2)}) copy-start(bf16[128,576]{0,1:T(8,128)(2,1)S(1)} %pad_maximum_fusion.3) | copy-start | bytes 442372
  76.8 0.7 copy-start.8
  76.8 0.8 copy-start.9
  77.3 1.0 copy-start.6
  79.4 12.0 %copy-start.4 = (f32[128,8,512]{2,0,1:T(8,128)}, f32[128,8,512]{2,0,1:T(8,128)S(1)}, u32[]{:S(2)}) copy-start(f32[128,8,512]{2,0,1:T(8,128)S(1)} %get-tuple-element.18) | copy-start | bytes 6291460
  87.5 1.3 copy-start.20
  92.1 4.2 %copy-start.3 = (bf16[128,2048]{1,0:T(8,128)(2,1)S(1)}, bf16[128,2048]{1,0:T(8,128)(2,1)}, u32[]{:S(2)}) copy-start(bf16[128,2048]{1,0:T(8,128)(2,1)} %param.18) | copy-start | bytes 1572868
  96.3 3.0 copy-start.18
  102.6 86.5 %all-to-all-start = ((bf16[16,64,2048]{2,1,0:T(8,128)(2,1)}), bf16[16,64,2048]{2,1,0:T(8,128)(2,1)}, u32[]{:S(2)}, u32[]{:S(2)}) async-start(bf16[16,64,2048]{2,1,0:T(8,128)(2,1)} %bitcast.81), calls=%async_computation | async-start | bytes 8388608 | tf_op jit(solution)/shard_map/all_to_all | solution.py:186
  108.3 88.7 %collective-permute-start = (bf16[2048,704]{0,1:T(8,128)(2,1)}, bf16[2048,704]{0,1:T(8,128)(2,1)}, u32[]{:S(2)}, u32[]{:S(2)}) collective-permute-start(bf16[2048,704]{0,1:T(8,128)(2,1)} %bitcast.86), channel_id=1, source_target_pairs={{0,1},{1,0},{2,3},{3,2},{4,5},{5,4},{6,7},{7,6},{8,9},{9,8},{10,11... | collective-permute-start | bytes 8650760 | tf_op jit(solution)/shard_map/ppermute | solution.py:12
  108.4 109.1 %collective-permute-start.2 = (bf16[704,2048]{1,0:T(8,128)(2,1)}, bf16[704,2048]{1,0:T(8,128)(2,1)}, u32[]{:S(2)}, u32[]{:S(2)}) collective-permute-start(bf16[704,2048]{1,0:T(8,128)(2,1)} %bitcast.87), channel_id=1, source_target_pairs={{0,1},{1,0},{2,3},{3,2},{4,5},{5,4},{6,7},{7,6},{8,9},{9,8},{10,11... | collective-permute-start | bytes 8650760 | tf_op jit(solution)/shard_map/ppermute | solution.py:12
  108.9 108.6 %collective-permute-start.1 = (bf16[2048,704]{0,1:T(8,128)(2,1)}, bf16[2048,704]{0,1:T(8,128)(2,1)}, u32[]{:S(2)}, u32[]{:S(2)}) collective-permute-start(bf16[2048,704]{0,1:T(8,128)(2,1)} %bitcast.88), channel_id=1, source_target_pairs={{0,1},{1,0},{2,3},{3,2},{4,5},{5,4},{6,7},{7,6},{8,9},{9,8},{10,11... | collective-permute-start | bytes 8650760 | tf_op jit(solution)/shard_map/ppermute | solution.py:12
  231.1 118.1 %copy-start.10 = (f32[128,16]{0,1:T(8,128)S(1)}, f32[128,16]{0,1:T(8,128)}, u32[]{:S(2)}) copy-start(f32[128,16]{0,1:T(8,128)} %get-tuple-element.2) | copy-start | bytes 24580
  231.1 118.1 %copy-start.12 = (f32[128,16]{0,1:T(8,128)S(1)}, f32[128,16]{0,1:T(8,128)}, u32[]{:S(2)}) copy-start(f32[128,16]{0,1:T(8,128)} %copy-done.11) | copy-start | bytes 24580
  231.1 118.1 %copy-start.14 = (pred[128,16]{0,1:T(8,128)(4,1)S(1)}, pred[128,16]{0,1:T(8,128)(4,1)}, u32[]{:S(2)}) copy-start(pred[128,16]{0,1:T(8,128)(4,1)} %copy-done.13) | copy-start | bytes 6148
  349.2 2.4 copy-start.1
Sparse Core Ops, SparseCore 0:
  10.8 54.7 all-gather.3
  67.7 16.1 all-gather.5

commit v2 on v1

--- a/solution.py
+++ b/solution.py
@@ -1,6 +1,10 @@
+import functools
+
 import jax
 import jax.numpy as jnp
 from jax import lax
+from jax.experimental import pallas as pl
+from jax.experimental.pallas import tpu as pltpu
 from jax.sharding import PartitionSpec as P
 
 EPSILON = 1e-06
@@ -74,12 +78,219 @@
     return (new_top, denominator, weighted)
 
 
-def route_tables(expert_ids, gate_weights, expert_count):
-    experts = jnp.arange(expert_count, dtype=jnp.int32)
-    named = expert_ids[:, :, None] == experts[None, None, :]
-    chosen_of = jnp.sum(named.astype(jnp.float32), axis=1)
-    gate_of = jnp.sum(jnp.where(named, gate_weights[:, :, None], 0.0), axis=1)
-    return (chosen_of, gate_of)
+PLANE = 4
+VMEM_BYTES = 40 * 1024 * 1024
+
+
+def place_of():
+    req = lax.axis_index("req")
+    sub = lax.axis_index("sub")
+    return (req // 2, req % 2, sub // 2, sub % 2)
+
+
+def line_device(step, line_count):
+    z, x, y, core = place_of()
+    return (((z + step + line_count) % line_count) * 2 + x, y * 2 + core)
+
+
+def mate_place(mate, x, y):
+    return (x + (mate // 2) * (1 - 2 * x), y + (mate % 2) * (1 - 2 * y))
+
+
+def plane_device(mate):
+    z, x, y, core = place_of()
+    other_x, other_y = mate_place(mate, x, y)
+    return (z * 2 + other_x, other_y * 2 + core)
+
+
+def remote(src, dst, send_sem, recv_sem, device):
+    return pltpu.make_async_remote_copy(
+        src_ref=src,
+        dst_ref=dst,
+        send_sem=send_sem,
+        recv_sem=recv_sem,
+        device_id=device,
+        device_id_type=pl.DeviceIdType.MESH,
+    )
+
+
+def greet(line_count):
+    barrier = pltpu.get_barrier_semaphore()
+    partners = [line_device(step, line_count) for step in range(1, line_count)]
+    partners += [plane_device(mate) for mate in range(1, PLANE)]
+    for partner in partners:
+        pl.semaphore_signal(
+            barrier, inc=1, device_id=partner, device_id_type=pl.DeviceIdType.MESH
+        )
+    pl.semaphore_wait(barrier, len(partners))
+
+
+def dispatch_kernel(
+    line_count, rows_ref, place_ref, out_ref, held, packed,
+    line_send, line_recv, plane_send, plane_recv, own_sem,
+):
+    greet(line_count)
+    along = {}
+    for step in range(1, line_count):
+        along[step] = remote(
+            rows_ref, held.at[step], line_send.at[step], line_recv.at[step],
+            line_device(step, line_count),
+        )
+        along[step].start()
+    started = []
+    for step in range(line_count):
+        if step:
+            along[step].wait_recv()
+        source = rows_ref[...] if step == 0 else held[step]
+        for mate in (3, 1, 2, 0):
+            packed[step, mate] = jnp.dot(
+                place_ref[step, mate], source, preferred_element_type=jnp.float32
+            ).astype(jnp.bfloat16)
+            if mate:
+                copy = remote(
+                    packed.at[step, mate], out_ref.at[step, mate],
+                    plane_send.at[step, mate], plane_recv.at[step, mate], plane_device(mate),
+                )
+            else:
+                copy = pltpu.make_async_copy(
+                    packed.at[step, 0], out_ref.at[step, 0], own_sem.at[step]
+                )
+            copy.start()
+            started.append(copy)
+    for step in range(1, line_count):
+        along[step].wait_send()
+    for copy in started:
+        copy.wait()
+
+
+def dispatch(rows, place):
+    line_count, _, capacity, row_count = place.shape
+    width = rows.shape[1]
+    return pl.pallas_call(
+        functools.partial(dispatch_kernel, line_count),
+        out_shape=jax.ShapeDtypeStruct((line_count, PLANE, capacity, width), jnp.bfloat16),
+        in_specs=[pl.BlockSpec(memory_space=pltpu.VMEM)] * 2,
+        out_specs=pl.BlockSpec(memory_space=pl.ANY),
+        scratch_shapes=[
+            pltpu.VMEM((line_count, row_count, width), jnp.bfloat16),
+            pltpu.VMEM((line_count, PLANE, capacity, width), jnp.bfloat16),
+            pltpu.SemaphoreType.DMA((line_count,)),
+            pltpu.SemaphoreType.DMA((line_count,)),
+            pltpu.SemaphoreType.DMA((line_count, PLANE)),
+            pltpu.SemaphoreType.DMA((line_count, PLANE)),
+            pltpu.SemaphoreType.DMA((line_count,)),
+        ],
+        compiler_params=pltpu.CompilerParams(
+            collective_id=0, has_side_effects=True, vmem_limit_bytes=VMEM_BYTES
+        ),
+    )(rows, place)
+
+
+def combine_kernel(
+    line_count, rows_ref, high_ref, low_ref, residual_ref, out_ref, back, leaving, landed, total,
+    plane_send, plane_recv, own_sem, line_send, line_recv,
+):
+    greet(line_count)
+    order = list(range(1, line_count)) + [0]
+    across = {}
+    for step in order:
+        for mate in (3, 1, 2, 0):
+            if mate:
+                copy = remote(
+                    rows_ref.at[step, mate], back.at[step, mate],
+                    plane_send.at[step, mate], plane_recv.at[step, mate], plane_device(mate),
+                )
+            else:
+                copy = pltpu.make_async_copy(
+                    rows_ref.at[step, 0], back.at[step, 0], own_sem.at[step]
+                )
+            copy.start()
+            across[step, mate] = copy
+    home = {}
+    for step in order:
+        for mate in range(PLANE):
+            across[step, mate].wait()
+        _, _, capacity, width = back.shape
+        expert_rows = back[step].reshape(PLANE * capacity, width)
+        mixed = jnp.dot(
+            high_ref[step], expert_rows, preferred_element_type=jnp.float32
+        ) + jnp.dot(low_ref[step], expert_rows, preferred_element_type=jnp.float32)
+        if step:
+            leaving[step] = mixed.astype(jnp.bfloat16)
+            home[step] = remote(
+                leaving.at[step], landed.at[step], line_send.at[step], line_recv.at[step],
+                line_device(-step, line_count),
+            )
+            home[step].start()
+        else:
+            total[...] = residual_ref[...] + mixed
+    for step in range(1, line_count):
+        home[step].wait()
+        total[...] += landed[step].astype(jnp.float32)
+    out_ref[...] = total[...].astype(jnp.bfloat16)
+
+
+def combine(expert_rows, mixing_high, mixing_low, residual):
+    line_count, _, capacity, width = expert_rows.shape
+    row_count = residual.shape[0]
+    vmem = pl.BlockSpec(memory_space=pltpu.VMEM)
+    return pl.pallas_call(
+        functools.partial(combine_kernel, line_count),
+        out_shape=jax.ShapeDtypeStruct((row_count, width), jnp.bfloat16),
+        in_specs=[pl.BlockSpec(memory_space=pl.ANY), vmem, vmem, vmem],
+        out_specs=vmem,
+        scratch_shapes=[
+            pltpu.VMEM((line_count, PLANE, capacity, width), jnp.bfloat16),
+            pltpu.VMEM((line_count, row_count, width), jnp.bfloat16),
+            pltpu.VMEM((line_count, row_count, width), jnp.bfloat16),
+            pltpu.VMEM((row_count, width), jnp.float32),
+            pltpu.SemaphoreType.DMA((line_count, PLANE)),
+            pltpu.SemaphoreType.DMA((line_count, PLANE)),
+            pltpu.SemaphoreType.DMA((line_count,)),
+            pltpu.SemaphoreType.DMA((line_count,)),
+            pltpu.SemaphoreType.DMA((line_count,)),
+        ],
+        compiler_params=pltpu.CompilerParams(
+            collective_id=1, has_side_effects=True, vmem_limit_bytes=VMEM_BYTES
+        ),
+    )(expert_rows, mixing_high, mixing_low, residual)
+
+
+def route_tables(expert_ids, gate_weights, capacity):
+    row_count, top_count = expert_ids.shape
+    line_count = lax.axis_size("req") // 2
+    z, x, y, _ = place_of()
+    both = jnp.concatenate([expert_ids.astype(jnp.float32), gate_weights], axis=1).T
+    every = lax.all_gather(both, "req", axis=0)
+    line = jnp.stack(
+        [
+            lax.dynamic_index_in_dim(
+                every, ((z - step + line_count) % line_count) * 2 + x, 0, keepdims=False
+            )
+            for step in range(line_count)
+        ]
+    )
+    experts = []
+    for mate in range(PLANE):
+        other_x, other_y = mate_place(mate, x, y)
+        experts.append(z * PLANE + other_x * 2 + other_y)
+    experts = jnp.stack(experts).astype(jnp.float32)
+    named = line[:, None, :top_count, :] == experts[None, :, None, None]
+    chosen = jnp.sum(named.astype(jnp.float32), axis=2)
+    gates = jnp.sum(jnp.where(named, line[:, None, top_count:, :], 0.0), axis=2)
+    row_order = jnp.arange(row_count, dtype=jnp.int32)
+    earlier = (row_order[:, None] < row_order[None, :]).astype(jnp.bfloat16)
+    slot_of = jnp.einsum(
+        "lmu,ut->lmt", chosen.astype(jnp.bfloat16), earlier, preferred_element_type=jnp.float32
+    )
+    slots = jnp.arange(capacity, dtype=jnp.float32)
+    at_slot = (slot_of[:, :, None, :] == slots[None, None, :, None]) & (chosen[:, :, None, :] > 0.0)
+    place = at_slot.astype(jnp.bfloat16)
+    mixing = jnp.where(at_slot, gates[:, :, None, :], 0.0)
+    mixing = mixing.reshape(line_count, PLANE * capacity, row_count).transpose(0, 2, 1)
+    mixing_high = mixing.astype(jnp.bfloat16)
+    mixing_low = (mixing - mixing_high.astype(jnp.float32)).astype(jnp.bfloat16)
+    return (place, mixing_high, mixing_low)
 
 
 def hidden_half(slot_rows, gate_half, up_half):
@@ -116,6 +327,10 @@
     device_count = lax.axis_size("req") * sub_count
     sub_index = lax.axis_index("sub")
     slab_rows = rows_dev * sub_count
+    top_count = expert_ids.shape[1]
+    expert_count = device_count // 2
+    capacity = 4 * rows_dev * top_count // (3 * expert_count)
+    place, mixing_high, mixing_low = route_tables(expert_ids, gate_weights, capacity)
     gate_other = swap_cores(w_gate[0])
     up_other = swap_cores(w_up[0])
     down_other = swap_cores(w_down[0])
@@ -168,49 +383,14 @@
         head_out, w_out, preferred_element_type=jnp.float32
     )
     normed_mid = rms_scale(residual, moe_gain).astype(jnp.bfloat16)
-    top_count = expert_ids.shape[1]
-    expert_count = device_count // 2
-    capacity = 4 * rows_dev * top_count // (3 * expert_count)
-    chosen_of, gate_of = route_tables(expert_ids, gate_weights, expert_count)
-    row_order = jnp.arange(rows_dev, dtype=jnp.int32)
-    earlier = (row_order[None, :] < row_order[:, None]).astype(jnp.bfloat16)
-    slot_of = jnp.dot(earlier, chosen_of.astype(jnp.bfloat16), preferred_element_type=jnp.float32)
-    slots = jnp.arange(capacity, dtype=jnp.float32)
-    at_slot = (slot_of[:, :, None] == slots[None, None, :]) & (chosen_of[:, :, None] > 0.0)
-    placing = at_slot.astype(jnp.bfloat16).reshape(rows_dev, expert_count * capacity)
-    mixing = jnp.where(at_slot, gate_of[:, :, None], 0.0).reshape(rows_dev, expert_count * capacity)
-    outbound = jnp.einsum(
-        "ts,td->sd", placing, normed_mid, preferred_element_type=jnp.float32
-    ).astype(jnp.bfloat16)
-    core_groups = [list(range(core, device_count, 2)) for core in range(2)]
-    arrived = lax.all_to_all(
-        outbound.reshape(expert_count, capacity, model_width),
-        ("req", "sub"),
-        split_axis=0,
-        concat_axis=0,
-        axis_index_groups=core_groups,
-        tiled=True,
-    ).reshape(-1, model_width)
+    arrived = dispatch(normed_mid, place).reshape(-1, model_width)
     expert_rows = jnp.dot(
         hidden_half(arrived, w_gate[0], w_up[0]), w_down[0], preferred_element_type=jnp.float32
     ) + jnp.dot(
         hidden_half(arrived, gate_other, up_other), down_other, preferred_element_type=jnp.float32
     )
-    expert_out = lax.all_to_all(
-        expert_rows.astype(jnp.bfloat16).reshape(expert_count, capacity, model_width),
-        ("req", "sub"),
-        split_axis=0,
-        concat_axis=0,
-        axis_index_groups=core_groups,
-        tiled=True,
-    )
-    expert_flat = expert_out.reshape(-1, model_width)
-    mixing_high = mixing.astype(jnp.bfloat16)
-    mixing_low = (mixing - mixing_high.astype(jnp.float32)).astype(jnp.bfloat16)
-    routed_sum = jnp.dot(mixing_high, expert_flat, preferred_element_type=jnp.float32) + jnp.dot(
-        mixing_low, expert_flat, preferred_element_type=jnp.float32
-    )
-    hidden_out = (residual + routed_sum).astype(jnp.bfloat16)
+    expert_out = expert_rows.astype(jnp.bfloat16).reshape(-1, PLANE, capacity, model_width)
+    hidden_out = combine(expert_out, mixing_high, mixing_low, residual)
     return (hidden_out, cache_rows)
 
 

time: 359 us -> 287 us (0.80)
  Pallas kernels: 0 us -> 138 us
  waiting for transfers between devices: 127 us -> 8.63 us
  blocking collectives: 126 us -> 40 us
  matrix products: 68.7 us -> 58.4 us
  local copies, waits for them, and re-layouts: 7.04 us -> 15.7 us
  starting transfers between devices: 6.41 us -> 1.11 us
    pallas_call x0 -> x2, Pallas kernels: none -> 138 us  [the longest x1 73.6 us: combine(): pl.pallas_call(functools.partial(combine_kernel, line_count), out_shape=j...]
    all_to_all x1 -> x0, blocking collectives: 118 us -> none  [local(): lax.all_to_all(expert_rows.astype(jnp.bfloat16).reshape(expert_count, cap...]
    all_to_all x1 -> x0, waiting for transfers between devices: 80.2 us -> none  [local(): lax.all_to_all(outbound.reshape(expert_count, capacity, model_width), ('r...]
    all_gather x1, waiting for transfers between devices: 41.9 us -> 3.78 us  [group_prefix(): every = lax.all_gather(mine, 'req', axis=0)]
    all_gather x0 -> x1, blocking collectives: none -> 32.1 us  [route_tables(): every = lax.all_gather(both, 'req', axis=0)]
    unnamed x43 -> x66, local copies, waits for them, and re-layouts: 1.59 us -> 7.77 us
    dot_general x4 -> x1, matrix products: 5.84 us -> 0.14 us  [route_tables(): jnp.einsum('lmu,ut->lmt', chosen.astype(jnp.bfloat16), earlier, preferred...]
    all_to_all x1 -> x0, starting transfers between devices: 5.68 us -> none  [local(): lax.all_to_all(outbound.reshape(expert_count, capacity, model_width), ('r...]
  transfers between devices with their start and end apart: 6 -> 5, of which waited for: 3 -> 2; matrix products, arithmetic and copies ran while one was open for 12% -> 21% of each run, Pallas kernels for 0% -> 22%
where the time goes in v2:
time: 287 us; the launch traced here: 286 us
  Pallas kernels  138 us (48%)
  matrix products  58.4 us (20%)
  blocking collectives  40 us (14%)
  between operations  17.2 us (6%)
  local copies, waits for them, and re-layouts  15.7 us (5%)
  waiting for transfers between devices  8.63 us (3%)
  other arithmetic  7.73 us (3%)
    pallas_call x1, Pallas kernels, combine(): pl.pallas_call(functools.partial(combine_kernel, line_count), out_shape=j...  73.6 us
    pallas_call x1, Pallas kernels, dispatch(): pl.pallas_call(functools.partial(dispatch_kernel, line_count), out_shape=...  64 us
    all_gather x1, blocking collectives, route_tables(): every = lax.all_gather(both, 'req', axis=0)  32.1 us
    dot_general x1, matrix products, local(): jnp.dot(hidden_half(arrived, gate_other, up_other), down_other, preferred...  13.8 us
    dot_general x1, matrix products, local(): jnp.dot(hidden_half(arrived, w_gate[0], w_up[0]), w_down[0], preferred_el...  12.6 us
    dot_general x2, matrix products, hidden_half(): jnp.dot(slot_rows, gate_half, preferred_element_type=jnp.float32)  11.4 us
    all_gather x1, blocking collectives, local(): key_block = lax.all_gather(cache_rows, 'sub', axis=0, tiled=True)  7.83 us
    unnamed x66, local copies, waits for them, and re-layouts  7.77 us
  transfers between devices with their start and end apart: 5, of which 2 were waited for; matrix products, arithmetic and copies ran while one was open for 21% of the time, Pallas kernels for 22%

profile of v2, /device:TPU:0, one launch (start us, length us, event | category | flops | bytes accessed | tf_op | source)
XLA Modules:
  0.0 286.3 jit_solution(8879634887926720173)
XLA Ops:
  7.2 1.9 constant_dynamic-slice_fusion.5
  10.8 1.3 dynamic_slice.34
  13.5 1.2 fusion.17
  14.7 4.8 %convolution_convert_fusion = bf16[128,1536]{1,0:T(8,128)(2,1)} fusion(bf16[2048,1536]{1,0:T(8,128)(2,1)} %param.20, bf16[128,2048]{1,0:T(8,128)(2,1)} %param.18, f32[2048]{0:T(1024)} %param.19, f32[128]{0:T(128)S(1)} %add_rsqrt_fusion.2), kind=kOutput, calls=%fused_computation.8 | convolution fusion | flops 806551552 | bytes 7217664 | tf_op jit(solution)/shard_map/dot_general | solution.py:352
  19.5 1.3 copy.53
  21.6 0.9 copy.74
  22.4 1.0 convert_element_type.80
  24.5 0.8 fusion.41
  26.5 32.1 %all-gather.2 = f32[8,12,128]{2,1,0:T(8,128)S(1)} all-gather(f32[1,12,128]{2,1,0:T(8,128)S(1)} %maximum_bitcast_fusion), channel_id=3, replica_groups=mesh['req'=8,'sub'=4] {'req'}, dimensions={0}, use_global_device_ids=true | all-gather | bytes 55296 | tf_op jit(solution)/shard_map/all_gather | solution.py:264
  60.9 0.7 fusion.40
  61.6 3.8 %all-gather.6.cloned.1.call-done = bf16[8,256,576]{1,2,0:T(8,128)(2,1)} async-done(((bf16[1,256,576]{1,2,0:T(8,128)(2,1)}), bf16[8,256,576]{1,2,0:T(8,128)(2,1)}) %all-gather.6.cloned.1.call-update) | async-done | bytes 2359312 | tf_op jit(solution)/shard_map/all_gather | solution.py:23
  65.4 1.7 constant_dynamic-slice_fusion.4
  67.1 7.8 %all_gather.18 = bf16[512,576]{0,1:T(8,128)(2,1)S(1)} all-gather(bf16[128,576]{0,1:T(8,128)(2,1)S(1)} %pad_maximum_fusion.3), channel_id=1, replica_groups=mesh['req'=8,'sub'=4] {'sub'}, dimensions={0}, use_global_device_ids=true | all-gather | bytes 737280 | tf_op jit(solution)/shard_map/all_gather | solution.py:371
  75.4 0.8 bitcast_convert_fusion.high_ref
  76.2 0.8 fusion.36.low_ref
  77.6 1.1 fusion.6
  78.7 4.8 %all-gather.8.cloned.1.call-done = bf16[1,1024,576]{1,2,0:T(8,128)(2,1)} async-done(((bf16[1,256,576]{1,2,0:T(8,128)(2,1)}), bf16[1,1024,576]{1,2,0:T(8,128)(2,1)}) %all-gather.8.cloned.1.call-update) | async-done | bytes 1179664 | tf_op jit(solution)/shard_map/all_gather | solution.py:25
  83.5 3.3 %multiply_reduce_fusion = (f32[128,8]{0,1:T(8,128)S(1)}, f32[128,8,1024]{2,0,1:T(8,128)S(1)}) fusion(bf16[1,1024,576]{1,2,0:T(8,128)(2,1)} %all-gather.8.cloned.1.call-done, bf16[128,8,32]{2,0,1:T(8,128)(2,1)} %copy-done.20, bf16[128,8,32]{2,0,1:T(8,128)(2,1)} %copy-done.19, bf16[128,8,512]{2,0,1:T(8,128)(2,1)S(1)} %fusion.10), kind=kOutput, calls=%fused_computation.2 | convolution fusion | flops 1213594624 | bytes 6557696 | tf_op jit(solution)/shard_map/thc,kc->thk/dot_general | solution.py:64
  86.8 0.9 fusion
  88.1 2.7 fusion.2
  91.5 4.2 %fusion.12 = bf16[8,128,128]{1,2,0:T(8,128)(2,1)S(1)} fusion(bf16[8,512,128]{2,1,0:T(8,128)(2,1)} %param.24, f32[128,8,512]{2,0,1:T(8,128)} %fusion.2, f32[128,8,512]{2,0,1:T(8,128)} %copy-done.10, f32[128,8]{0,1:T(8,128)S(1)} %get-tuple-element.4, f32[128,8]{0,1:T(8,128)S(1)} %get-tuple-element.17, f32[128,8]{0,1:T(8,128)S(1)} %get-tuple-element.5, ...), kind=kOutput, calls=%fused_computation.25 | convolution fusion | flops 676462592 | bytes 6111232 | tf_op jit(solution)/shard_map/thc,hcv->thv/dot_general | solution.py:378
  95.7 3.0 %multiply_reduce_fusion.1 = (f32[128]{0:T(128)S(1)}, f32[128,2048]{1,0:T(8,128)S(1)}) fusion(bf16[128,1024]{0,1:T(8,128)(2,1)S(1)} %bitcast.92, bf16[1024,2048]{1,0:T(8,128)(2,1)} %param.25, bf16[128,2048]{1,0:T(8,128)(2,1)S(1)} %copy-done.7), kind=kOutput, calls=%fused_computation.33 | convolution fusion | flops 537919360 | bytes 6029824 | tf_op jit(solution)/shard_map/dot_general | solution.py:382
  98.9 64.0 %shard_map.185 = bf16[4,4,64,2048]{3,2,1,0:T(8,128)(2,1)S(1)} custom-call(bf16[128,2048]{1,0:T(8,128)(2,1)S(1)} %multiply_convert_fusion.3.rows_ref, bf16[4,4,64,128]{3,2,1,0:T(8,128)(2,1)S(1)} %fusion.38.place_ref), custom_call_target="tpu_custom_call" | custom-call | tf_op jit(solution)/shard_map/pallas_call | solution.py:169
  162.9 4.8 %fusion.56 = f32[1024,704]{0,1:T(8,128)} fusion(bf16[1024,2048]{1,0:T(8,128)(2,1)S(1)} %bitcast.82, bf16[1,2048,704]{1,2,0:T(8,128)(2,1)S(1)} %copy-done.29), kind=kOutput, calls=%fused_computation.106 | convolution fusion | flops 2952790016 | bytes 9961472 | tf_op jit(solution)/shard_map/dot_general | solution.py:297
  167.7 6.6 %fusion.71 = f32[1024,704]{0,1:T(8,128)} fusion(bf16[1024,2048]{1,0:T(8,128)(2,1)S(1)} %bitcast.83, bf16[2048,704]{0,1:T(8,128)(2,1)} %collective-permute-done), kind=kOutput, calls=%fused_computation.117 | convolution fusion | flops 2952790016 | bytes 9961472 | tf_op jit(solution)/shard_map/dot_general | solution.py:297
  174.3 12.6 %fusion.33 = f32[1024,2048]{1,0:T(8,128)} fusion(f32[1024,704]{0,1:T(8,128)} %fusion.56, bf16[1024,2048]{1,0:T(8,128)(2,1)} %bitcast.84, bf16[1,704,2048]{2,1,0:T(8,128)(2,1)} %param.29, bf16[1,2048,704]{1,2,0:T(8,128)(2,1)} %param.28), kind=kOutput, calls=%fused_computation.42 | convolution fusion | flops 5909905408 | bytes 21233664 | tf_op jit(solution)/shard_map/dot_general | solution.py:387
  187.0 13.8 %add_convert_fusion = bf16[1024,2048]{1,0:T(8,128)(2,1)} fusion(f32[1024,2048]{1,0:T(8,128)} %fusion.33, bf16[704,2048]{1,0:T(8,128)(2,1)} %collective-permute-done.2, f32[1024,704]{0,1:T(8,128)} %fusion.71, bf16[1024,2048]{1,0:T(8,128)(2,1)} %bitcast.85, bf16[2048,704]{0,1:T(8,128)(2,1)} %collective-permute-done.1), kind=kOutput, calls=%fused_computation | convolution fusion | flops 5914099712 | bytes 25427968 | tf_op jit(solution)/shard_map/dot_general | solution.py:389
  200.8 2.3 copy-done.3
  203.2 0.9 copy-done.4
  204.1 0.9 copy-done.5
  205.1 73.6 %shard_map.186 = bf16[128,2048]{1,0:T(8,128)(2,1)S(1)} custom-call(bf16[4,4,64,2048]{3,2,1,0:T(8,128)(2,1)S(1)} %bitcast.86, bf16[4,128,256]{2,1,0:T(8,128)(2,1)S(1)} %copy-done.4, bf16[4,128,256]{2,1,0:T(8,128)(2,1)S(1)} %copy-done.5, f32[128,2048]{1,0:T(8,128)S(1)} %get-tuple-element.26.residual_ref), custom_call_target="tpu_custom_call" | custom-call | tf_op jit(solution)/shard_map/pallas_call | solution.py:237
  278.7 0.8 copy.77
  (115 shorter events, 7.7 us)
Async XLA Ops:
  7.2 17.3 %copy-start = (bf16[2048,576]{0,1:T(8,128)(2,1)S(1)}, bf16[2048,576]{0,1:T(8,128)(2,1)}, u32[]{:S(2)}) copy-start(bf16[2048,576]{0,1:T(8,128)(2,1)} %param.21) | copy-start | bytes 7077892
  7.2 58.2 %all-gather.6.cloned.1.call-start = ((), (), s32[]{:S(2)}) async-start(), calls=%async_computation | async-start | bytes 2654208 | tf_op jit(solution)/shard_map/all_gather | solution.py:23
  9.1 74.4 %all-gather.8.cloned.1.call-start = ((), (), s32[]{:S(2)}) async-start(), calls=%async_computation.1 | async-start | bytes 1474560 | tf_op jit(solution)/shard_map/all_gather | solution.py:25
  9.2 177.8 %collective-permute-start.2 = (bf16[704,2048]{1,0:T(8,128)(2,1)}, bf16[704,2048]{1,0:T(8,128)(2,1)}, u32[]{:S(2)}, u32[]{:S(2)}) collective-permute-start(bf16[704,2048]{1,0:T(8,128)(2,1)} %bitcast.94), channel_id=1, source_target_pairs={{0,1},{1,0},{2,3},{3,2},{4,5},{5,4},{6,7},{7,6},{8,9},{9,8},{10,11... | collective-permute-start | bytes 8650760 | tf_op jit(solution)/shard_map/ppermute | solution.py:16
  9.7 158.0 %collective-permute-start = (bf16[2048,704]{0,1:T(8,128)(2,1)}, bf16[2048,704]{0,1:T(8,128)(2,1)}, u32[]{:S(2)}, u32[]{:S(2)}) collective-permute-start(bf16[2048,704]{0,1:T(8,128)(2,1)} %bitcast.93), channel_id=1, source_target_pairs={{0,1},{1,0},{2,3},{3,2},{4,5},{5,4},{6,7},{7,6},{8,9},{9,8},{10,11... | collective-permute-start | bytes 8650760 | tf_op jit(solution)/shard_map/ppermute | solution.py:16
  9.8 177.2 %collective-permute-start.1 = (bf16[2048,704]{0,1:T(8,128)(2,1)}, bf16[2048,704]{0,1:T(8,128)(2,1)}, u32[]{:S(2)}, u32[]{:S(2)}) collective-permute-start(bf16[2048,704]{0,1:T(8,128)(2,1)} %bitcast.95), channel_id=1, source_target_pairs={{0,1},{1,0},{2,3},{3,2},{4,5},{5,4},{6,7},{7,6},{8,9},{9,8},{10,11... | collective-permute-start | bytes 8650760 | tf_op jit(solution)/shard_map/ppermute | solution.py:16
  14.7 8.7 %copy-start.31 = (s32[1,3]{1,0:T(1,128)S(1)}, s32[1,3]{1,0:T(1,128)}, u32[]{:S(2)}) copy-start(s32[1,3]{1,0:T(1,128)} %param.32) | copy-start | bytes 40
  14.7 9.8 %copy-start.6 = (bf16[128,2048]{1,0:T(8,128)(2,1)S(1)}, bf16[128,2048]{1,0:T(8,128)(2,1)}, u32[]{:S(2)}) copy-start(bf16[128,2048]{1,0:T(8,128)(2,1)} %param.18) | copy-start | bytes 1572868
  14.7 9.8 %copy-start.21 = (f32[2048]{0:T(1024)S(1)}, f32[2048]{0:T(1024)}, u32[]{:S(2)}) copy-start(f32[2048]{0:T(1024)} %param.19) | copy-start | bytes 24580
  19.5 7.0 %copy-start.25 = (s32[128,6]{0,1:T(8,128)S(1)}, s32[128,6]{0,1:T(8,128)}, u32[]{:S(2)}) copy-start(s32[128,6]{0,1:T(8,128)} %param.30) | copy-start | bytes 9220
  19.5 7.0 %copy-start.26 = (f32[128,6]{0,1:T(8,128)S(1)}, f32[128,6]{0,1:T(8,128)}, u32[]{:S(2)}) copy-start(f32[128,6]{0,1:T(8,128)} %param.31) | copy-start | bytes 9220
  26.1 34.6 %copy-start.27 = (f32[512]{0:T(512)S(1)}, f32[512]{0:T(512)}, u32[]{:S(2)}) copy-start(f32[512]{0:T(512)} %param.22) | copy-start | bytes 6148
  26.1 34.8 %copy-start.23 = (s32[512]{0:T(512)S(1)}, s32[512]{0:T(512)}, u32[]{:S(2)}) copy-start(s32[512]{0:T(512)} %copy-done.22) | copy-start | bytes 6148
  26.1 34.8 %copy-start.28 = (s32[128]{0:T(128)S(1)}, s32[128]{0:T(128)}, u32[]{:S(2)}) copy-start(s32[128]{0:T(128)} %dynamic_slice.36) | copy-start | bytes 1540
  26.2 34.4 %copy-start.9 = (f32[128,576]{0,1:T(8,128)S(1)}, f32[128,576]{0,1:T(8,128)}, u32[]{:S(2)}) copy-start(f32[128,576]{0,1:T(8,128)} %copy-done.8) | copy-start | bytes 884740
  60.9 16.2 %copy-start.16 = (bf16[128,576]{0,1:T(8,128)(2,1)}, bf16[128,576]{0,1:T(8,128)(2,1)S(1)}, u32[]{:S(2)}) copy-start(bf16[128,576]{0,1:T(8,128)(2,1)S(1)} %pad_maximum_fusion.3) | copy-start | bytes 442372
  67.1 9.9 %copy-start.12 = (bf16[128,1536]{0,1:T(8,128)(2,1)S(1)}, bf16[128,1536]{0,1:T(8,128)(2,1)}, u32[]{:S(2)}) copy-start(bf16[128,1536]{0,1:T(8,128)(2,1)} %copy-done.11) | copy-start | bytes 1179652
  67.1 9.9 %copy-start.13 = (bf16[8,128,512]{2,1,0:T(8,128)(2,1)S(1)}, bf16[8,128,512]{2,1,0:T(8,128)(2,1)}, u32[]{:S(2)}) copy-start(bf16[8,128,512]{2,1,0:T(8,128)(2,1)} %param.23) | copy-start | bytes 3145732
  75.0 2.5 copy-start.14
  75.3 2.2 copy-start.19
  75.4 2.2 copy-start.20
  75.4 2.2 copy-start.17
  78.7 12.1 %copy-start.10 = (f32[128,8,512]{2,0,1:T(8,128)}, f32[128,8,512]{2,0,1:T(8,128)S(1)}, u32[]{:S(2)}) copy-start(f32[128,8,512]{2,0,1:T(8,128)S(1)} %get-tuple-element.24) | copy-start | bytes 6291460
  86.8 1.3 copy-start.30
  88.1 2.7 copy-start.18
  88.1 3.4 %copy-start.15 = (bf16[512,576]{0,1:T(8,128)(2,1)S(1)}, bf16[512,576]{0,1:T(8,128)(2,1)}, u32[]{:S(2)}) copy-start(bf16[512,576]{0,1:T(8,128)(2,1)} %copy-done.14) | copy-start | bytes 1769476
  91.5 4.2 %copy-start.7 = (bf16[128,2048]{1,0:T(8,128)(2,1)S(1)}, bf16[128,2048]{1,0:T(8,128)(2,1)}, u32[]{:S(2)}) copy-start(bf16[128,2048]{1,0:T(8,128)(2,1)} %param.18) | copy-start | bytes 1572868
  95.7 3.0 %copy-start.24 = (f32[2048]{0:T(1024)S(1)}, f32[2048]{0:T(1024)}, u32[]{:S(2)}) copy-start(f32[2048]{0:T(1024)} %param.26) | copy-start | bytes 24580
  98.9 64.1 %copy-start.29 = (bf16[1,2048,704]{1,2,0:T(8,128)(2,1)S(1)}, bf16[1,2048,704]{1,2,0:T(8,128)(2,1)}, u32[]{:S(2)}) copy-start(bf16[1,2048,704]{1,2,0:T(8,128)(2,1)} %param.27) | copy-start | bytes 8650756
  162.9 4.8 %copy-start.2 = (bf16[4,4,64,2048]{3,2,1,0:T(8,128)(2,1)}, bf16[4,4,64,2048]{3,2,1,0:T(8,128)(2,1)S(1)}, u32[]{:S(2)}) copy-start(bf16[4,4,64,2048]{3,2,1,0:T(8,128)(2,1)S(1)} %shard_map.185) | copy-start | bytes 12582916
  200.8 78.6 %copy-start.1 = (bf16[2048,576]{0,1:T(8,128)(2,1)S(1)}, bf16[2048,576]{0,1:T(8,128)(2,1)}, u32[]{:S(2)}) copy-start(bf16[2048,576]{0,1:T(8,128)(2,1)} %param.21) | copy-start | bytes 7077892
  200.8 2.3 copy-start.3
  (5 other events, 4.2 us)
Sparse Core Ops, SparseCore 0:
  10.2 55.1 all-gather.5
  67.3 16.1 all-gather.7
